TPU v7x, 512 devices: a whole 4x8x8 slice. The times are simulated.
512 devices in a mesh: section: 16 (over z_lo, x), feat: 32 (over y, z_hi, core).
Axes of the slice: x: 4, y: 8, z: 8 (z_hi: 2, z_lo: 4; z = z_hi * 4 + z_lo), core: 2. Of those that a mesh axis runs over, the one named last changes fastest.
Arguments:
- decoders: bfloat16 [16, 4096, 4608], P('section', 'feat'), may hold values from -0.09375 to 0.09375
- encoders: bfloat16 [16, 4096, 4608], P('section', 'feat'), may hold values from -6 to 6
- out_proj: bfloat16 [16, 4096, 4608], P('section', 'feat'), may hold values from -0.09375 to 0.09375
- value_proj: bfloat16 [16, 4608, 4096], P('section', None, 'feat'), may hold values from -0.09375 to 0.09375
- attention: float32 [16, 32, 16, 16], P('section', 'feat'), may hold values from 0 to 1, as said below
- norm_scale: float32 [16, 16], P('section'), may hold values from 0.05 to 0.5
- act_ids: int32 [16, 4096], P('section'), may hold values from 0 to 4095, as said below
- act_values: float32 [16, 4096], P('section', 'feat'), may hold values from 0.1 to 10
- target_ids: int32 [64], P('section'), may hold values from 0 to 4095
- target_pos: int32 [64], P('section'), may hold values from 0 to 15
Outputs:
- edges: float32 [16, 64, 4096], P('section', None, 'feat')
Inputs may be any that keep to these rules, and one draw needn't show every extreme that they name: Every row attention[l, h, p, :] is nonnegative, zero at keys after p, and sums to one. `act_ids`: A feature id f is held by shard f // 128 of feat. In each aligned block of 128 entries of a layer (the entries of one device), at most 8 ids lie in one shard, and in every block some shard has exactly 8.
All inputs are finite; a program needn't handle non-finite values.
Results may differ from a plain program's by a relative error of at most 0.015.
Values may be sent and summed in bfloat16 or wider, within the bound.
No kernel may reach another device: no remote copies, remote signals or barrier semaphores. Data moves between devices by JAX's collectives and lax.ppermute only.
A program may use at most 64 MiB of HBM per device.

v0:
```python
import jax
import jax.numpy as jnp
from jax import lax
from jax.sharding import PartitionSpec as P

K_ACT = 256


def shifted(shard, axis, by):
    length = lax.axis_size(axis)
    pairs = [(i, i + by) for i in range(length) if 0 <= i + by < length]
    return lax.ppermute(shard, axis, pairs)


def per_device(
    decoders,
    encoders,
    out_proj,
    value_proj,
    attention,
    norm_scale,
    act_ids,
    act_values,
    target_ids,
    target_pos,
):
    feat_count = lax.axis_size("feat")
    section_count = lax.axis_size("section")
    feat_index = lax.axis_index("feat")
    section_index = lax.axis_index("section")
    dec_table = decoders[0]
    enc_table = encoders[0]
    out_weight = out_proj[0]
    value_weight = value_proj[0]
    mixing = attention[0, 0]
    scales = norm_scale[0]
    act_weights = act_values[0]
    feat_rows = dec_table.shape[0]
    model_width = dec_table.shape[1]
    head_width = out_weight.shape[0]
    seq_len = mixing.shape[0]
    batch_size = target_ids.shape[0]
    entries_dev = act_weights.shape[0]
    slot_count = 2 * entries_dev // feat_count
    rows_all = batch_size * seq_len
    rows_dev = rows_all // feat_count
    ids_blocks = act_ids[0].reshape(feat_count, entries_dev)
    owner_ids = ids_blocks // feat_rows
    local_ids = ids_blocks % feat_rows
    owned_mask = (owner_ids == feat_index).astype(jnp.int32)
    slot_rank = jnp.cumsum(owned_mask, axis=1) - 1
    slot_iota = jnp.arange(slot_count, dtype=jnp.int32)
    selected = owned_mask[:, None, :] * (slot_rank[:, None, :] == slot_iota[None, :, None]).astype(
        jnp.int32
    )
    source_row = jnp.sum(selected * local_ids[:, None, :], axis=2)
    is_filled = jnp.sum(selected, axis=2)
    entry_iota = jnp.arange(entries_dev, dtype=jnp.int32)
    outgoing = jnp.take(dec_table, source_row.reshape(-1), axis=0).reshape(
        feat_count, slot_count, model_width
    )
    outgoing = jnp.where(is_filled[:, :, None] > 0, outgoing, jnp.zeros_like(outgoing))
    own_owner = lax.dynamic_index_in_dim(owner_ids, feat_index, 0, keepdims=False)
    earlier = (entry_iota[None, :] < entry_iota[:, None]).astype(jnp.int32)
    same_owner = (own_owner[:, None] == own_owner[None, :]).astype(jnp.int32)
    own_rank = jnp.sum(earlier * same_owner, axis=1)
    flat_index = own_owner * slot_count + own_rank
    positions = jnp.arange(seq_len, dtype=jnp.int32)
    incoming = lax.all_to_all(outgoing, "feat", split_axis=0, concat_axis=0, tiled=True)
    partners = jnp.take(incoming.reshape(feat_count * slot_count, model_width), flat_index, axis=0)
    own_pos = (feat_index * entries_dev + entry_iota) // K_ACT
    edge_pick = (positions[:, None] == own_pos[None, :]).astype(jnp.float32)
    feat_iota = jnp.arange(feat_rows, dtype=jnp.int32)
    target_pick = ((target_ids - feat_index * feat_rows)[:, None] == feat_iota[None, :]).astype(
        jnp.bfloat16
    )
    enc_part = jnp.dot(target_pick, enc_table, preferred_element_type=jnp.float32)
    enc_full = lax.psum(enc_part.astype(jnp.bfloat16), "feat").astype(jnp.float32)
    row_iota = feat_index * rows_dev + jnp.arange(rows_dev, dtype=jnp.int32)
    row_target = row_iota // seq_len
    row_pos = row_iota % seq_len
    target_onehot = (
        row_target[:, None] == jnp.arange(batch_size, dtype=jnp.int32)[None, :]
    ).astype(jnp.float32)
    row_enc = jnp.dot(target_onehot, enc_full, precision=lax.Precision.HIGHEST)
    row_hit = jnp.sum(
        target_onehot * (row_pos[:, None] == target_pos[None, :]).astype(jnp.float32), axis=1
    )
    start_rows = row_enc * row_hit[:, None]
    scale_rows = jnp.tile(scales, batch_size)

    def produce(shard_rows):
        head_part = lax.dot_general(
            shard_rows, out_weight, (((1,), (1,)), ((), ())), preferred_element_type=jnp.float32
        )
        edge_part = lax.dot_general(
            shard_rows, partners, (((1,), (1,)), ((), ())), preferred_element_type=jnp.float32
        )
        return jnp.concatenate([head_part, edge_part], axis=1)

    def gathered_products(adjoint_rows):
        joined = produce(
            lax.all_gather(adjoint_rows.astype(jnp.bfloat16), "feat", axis=0, tiled=True)
        )
        return (joined[:, :head_width], joined[:, head_width:])

    def record(edges_out, edge_raw, step_num):
        edge_vals = jnp.sum(edge_raw.reshape(batch_size, seq_len, -1) * edge_pick[None], axis=1)
        edge_vals = edge_vals * act_weights[None, :]
        batch_num = section_index + step_num
        in_range = batch_num < section_count
        row_start = jnp.minimum(batch_num, section_count - 1) * batch_size
        current = lax.dynamic_slice_in_dim(edges_out, row_start, batch_size, 0)
        updated = jnp.where(in_range, edge_vals, current)
        return lax.dynamic_update_slice_in_dim(edges_out, updated, row_start, 0)

    def propagate(adjoint_rows, head_grad):
        mixed_rows = jnp.einsum(
            "pq,tph->tqh", mixing, head_grad.reshape(batch_size, seq_len, head_width)
        )
        mixed_rows = mixed_rows.astype(jnp.bfloat16).reshape(rows_all, head_width)
        head_term = lax.dot_general(
            mixed_rows, value_weight, (((1,), (1,)), ((), ())), preferred_element_type=jnp.float32
        )
        head_term = (head_term * scale_rows[:, None]).astype(jnp.bfloat16)
        head_parts = lax.all_to_all(
            head_term.reshape(feat_count, rows_dev, model_width),
            "feat",
            split_axis=0,
            concat_axis=0,
            tiled=True,
        )
        return adjoint_rows + jnp.sum(head_parts.astype(jnp.float32), axis=0)

    def one_hop(step_num, loop_state):
        adjoint_rows, edges_out = loop_state
        head_grad, edge_raw = gathered_products(adjoint_rows)
        edges_out = record(edges_out, edge_raw, step_num)
        adjoint_rows = propagate(adjoint_rows, head_grad)
        adjoint_rows = shifted(adjoint_rows, "section", -1)
        return (adjoint_rows, edges_out)

    blank_edges = jnp.zeros((batch_size * section_count, entries_dev), jnp.float32)
    adjoint_rows, edges_out = lax.fori_loop(
        0, section_count - 1, one_hop, (start_rows, blank_edges)
    )
    unused, edge_raw = gathered_products(adjoint_rows)
    edges_out = record(edges_out, edge_raw, section_count - 1)
    return edges_out[None]


def solution(mesh):
    in_specs = (
        P("section", "feat", None),
        P("section", "feat", None),
        P("section", "feat", None),
        P("section", None, "feat"),
        P("section", "feat", None, None),
        P("section", None),
        P("section", None),
        P("section", "feat"),
        P("section"),
        P("section"),
    )
    out_specs = P("section", None, "feat")
    return jax.shard_map(
        per_device, mesh=mesh, in_specs=in_specs, out_specs=out_specs, check_vma=False
    )
```

profile of v0, /device:TPU:7, one launch (start us, length us, event | category | flops | bytes accessed | tf_op | source)
XLA Modules:
  0.0 1708.6 jit_solution(6113719031879558442)
XLA Ops:
  7.6 16.5 all-to-all-start.1
  27.0 205.2 %psum.7 = bf16[4,4608]{1,0:T(4,128)(2,1)} all-reduce(bf16[4,4608]{1,0:T(4,128)(2,1)} %convolution_convert_fusion.1), channel_id=1, replica_groups=mesh['section'=16,'feat'=32] {'feat'}, use_global_device_ids=true, to_apply=%region_0.1 | all-reduce | flops 18432 | bytes 73728 | tf_op jit(solution)/shard_map/psum | solution.py:78
  243.1 1407.9 %while.16 = (s32[]{:T(128)}, f32[2,4608]{1,0:T(2,128)S(1)}, f32[64,128]{1,0:T(8,128)}, bf16[128,4608]{1,0:T(8,128)(2,1)}, bf16[16,16]{0,1:T(8,128)(2,1)S(1)}, /*...) while((s32[]{:T(128)}, f32[2,4608]{1,0:T(2,128)S(1)}, ...), condition=%wide.region_9.10_spmd.clone, body=%wide.region_6.9_spmd.clone.sunk | while | flops 227964416 | bytes 15944625 | solution.py:144
  243.7 56.5 %all-gather.4 = bf16[32,2,4608]{2,1,0:T(2,128)(2,1)S(1)} all-gather(bf16[1,2,4608]{2,1,0:T(2,128)(2,1)S(1)} %convert_bitcast_fusion.3), channel_id=1, replica_groups=mesh['section'=16,'feat'=32] {'feat'}, dimensions={0}, use_global_device_ids=true | all-gather | bytes 608256 | tf_op jit(solution)/shard_map/while/body/eval_jaxpr/all_gather | solution.py:103
  304.7 10.4 all-to-all-start
  316.3 19.1 %all-to-all-done = bf16[32,2,4608]{2,1,0:T(2,128)(2,1)S(1)} async-done(((bf16[32,2,4608]{2,1,0:T(2,128)(2,1)}), bf16[32,2,4608]{2,1,0:T(2,128)(2,1)S(1)}, u32[]{:S(2)}, u32[]{:S(2)}) %all-to-all-start) | async-done | bytes 589856 | tf_op jit(solution)/shard_map/while/body/eval_jaxpr/all_to_all | solution.py:126
  340.3 3.1 collective-permute-done
  344.0 53.4 %all-gather.4 = bf16[32,2,4608]{2,1,0:T(2,128)(2,1)S(1)} all-gather(bf16[1,2,4608]{2,1,0:T(2,128)(2,1)S(1)} %convert_bitcast_fusion.3), channel_id=1, replica_groups=mesh['section'=16,'feat'=32] {'feat'}, dimensions={0}, use_global_device_ids=true | all-gather | bytes 608256 | tf_op jit(solution)/shard_map/while/body/eval_jaxpr/all_gather | solution.py:103
  402.0 7.1 all-to-all-start
  410.3 18.7 %all-to-all-done = bf16[32,2,4608]{2,1,0:T(2,128)(2,1)S(1)} async-done(((bf16[32,2,4608]{2,1,0:T(2,128)(2,1)}), bf16[32,2,4608]{2,1,0:T(2,128)(2,1)S(1)}, u32[]{:S(2)}, u32[]{:S(2)}) %all-to-all-start) | async-done | bytes 589856 | tf_op jit(solution)/shard_map/while/body/eval_jaxpr/all_to_all | solution.py:126
  433.4 3.6 collective-permute-done
  437.7 54.1 %all-gather.4 = bf16[32,2,4608]{2,1,0:T(2,128)(2,1)S(1)} all-gather(bf16[1,2,4608]{2,1,0:T(2,128)(2,1)S(1)} %convert_bitcast_fusion.3), channel_id=1, replica_groups=mesh['section'=16,'feat'=32] {'feat'}, dimensions={0}, use_global_device_ids=true | all-gather | bytes 608256 | tf_op jit(solution)/shard_map/while/body/eval_jaxpr/all_gather | solution.py:103
  496.3 6.3 all-to-all-start
  503.8 18.6 %all-to-all-done = bf16[32,2,4608]{2,1,0:T(2,128)(2,1)S(1)} async-done(((bf16[32,2,4608]{2,1,0:T(2,128)(2,1)}), bf16[32,2,4608]{2,1,0:T(2,128)(2,1)S(1)}, u32[]{:S(2)}, u32[]{:S(2)}) %all-to-all-start) | async-done | bytes 589856 | tf_op jit(solution)/shard_map/while/body/eval_jaxpr/all_to_all | solution.py:126
  526.9 3.6 collective-permute-done
  531.1 54.1 %all-gather.4 = bf16[32,2,4608]{2,1,0:T(2,128)(2,1)S(1)} all-gather(bf16[1,2,4608]{2,1,0:T(2,128)(2,1)S(1)} %convert_bitcast_fusion.3), channel_id=1, replica_groups=mesh['section'=16,'feat'=32] {'feat'}, dimensions={0}, use_global_device_ids=true | all-gather | bytes 608256 | tf_op jit(solution)/shard_map/while/body/eval_jaxpr/all_gather | solution.py:103
  589.7 6.2 all-to-all-start
  597.1 18.7 %all-to-all-done = bf16[32,2,4608]{2,1,0:T(2,128)(2,1)S(1)} async-done(((bf16[32,2,4608]{2,1,0:T(2,128)(2,1)}), bf16[32,2,4608]{2,1,0:T(2,128)(2,1)S(1)}, u32[]{:S(2)}, u32[]{:S(2)}) %all-to-all-start) | async-done | bytes 589856 | tf_op jit(solution)/shard_map/while/body/eval_jaxpr/all_to_all | solution.py:126
  620.2 3.6 collective-permute-done
  624.5 54.1 %all-gather.4 = bf16[32,2,4608]{2,1,0:T(2,128)(2,1)S(1)} all-gather(bf16[1,2,4608]{2,1,0:T(2,128)(2,1)S(1)} %convert_bitcast_fusion.3), channel_id=1, replica_groups=mesh['section'=16,'feat'=32] {'feat'}, dimensions={0}, use_global_device_ids=true | all-gather | bytes 608256 | tf_op jit(solution)/shard_map/while/body/eval_jaxpr/all_gather | solution.py:103
  683.1 6.2 all-to-all-start
  690.5 18.7 %all-to-all-done = bf16[32,2,4608]{2,1,0:T(2,128)(2,1)S(1)} async-done(((bf16[32,2,4608]{2,1,0:T(2,128)(2,1)}), bf16[32,2,4608]{2,1,0:T(2,128)(2,1)S(1)}, u32[]{:S(2)}, u32[]{:S(2)}) %all-to-all-start) | async-done | bytes 589856 | tf_op jit(solution)/shard_map/while/body/eval_jaxpr/all_to_all | solution.py:126
  713.6 3.6 collective-permute-done
  717.8 54.2 %all-gather.4 = bf16[32,2,4608]{2,1,0:T(2,128)(2,1)S(1)} all-gather(bf16[1,2,4608]{2,1,0:T(2,128)(2,1)S(1)} %convert_bitcast_fusion.3), channel_id=1, replica_groups=mesh['section'=16,'feat'=32] {'feat'}, dimensions={0}, use_global_device_ids=true | all-gather | bytes 608256 | tf_op jit(solution)/shard_map/while/body/eval_jaxpr/all_gather | solution.py:103
  776.6 6.1 all-to-all-start
  783.8 18.7 %all-to-all-done = bf16[32,2,4608]{2,1,0:T(2,128)(2,1)S(1)} async-done(((bf16[32,2,4608]{2,1,0:T(2,128)(2,1)}), bf16[32,2,4608]{2,1,0:T(2,128)(2,1)S(1)}, u32[]{:S(2)}, u32[]{:S(2)}) %all-to-all-start) | async-done | bytes 589856 | tf_op jit(solution)/shard_map/while/body/eval_jaxpr/all_to_all | solution.py:126
  806.9 3.7 collective-permute-done
  811.2 54.2 %all-gather.4 = bf16[32,2,4608]{2,1,0:T(2,128)(2,1)S(1)} all-gather(bf16[1,2,4608]{2,1,0:T(2,128)(2,1)S(1)} %convert_bitcast_fusion.3), channel_id=1, replica_groups=mesh['section'=16,'feat'=32] {'feat'}, dimensions={0}, use_global_device_ids=true | all-gather | bytes 608256 | tf_op jit(solution)/shard_map/while/body/eval_jaxpr/all_gather | solution.py:103
  870.0 6.1 all-to-all-start
  877.2 18.7 %all-to-all-done = bf16[32,2,4608]{2,1,0:T(2,128)(2,1)S(1)} async-done(((bf16[32,2,4608]{2,1,0:T(2,128)(2,1)}), bf16[32,2,4608]{2,1,0:T(2,128)(2,1)S(1)}, u32[]{:S(2)}, u32[]{:S(2)}) %all-to-all-start) | async-done | bytes 589856 | tf_op jit(solution)/shard_map/while/body/eval_jaxpr/all_to_all | solution.py:126
  900.3 3.6 collective-permute-done
  904.6 54.2 %all-gather.4 = bf16[32,2,4608]{2,1,0:T(2,128)(2,1)S(1)} all-gather(bf16[1,2,4608]{2,1,0:T(2,128)(2,1)S(1)} %convert_bitcast_fusion.3), channel_id=1, replica_groups=mesh['section'=16,'feat'=32] {'feat'}, dimensions={0}, use_global_device_ids=true | all-gather | bytes 608256 | tf_op jit(solution)/shard_map/while/body/eval_jaxpr/all_gather | solution.py:103
  963.3 6.1 all-to-all-start
  970.6 18.7 %all-to-all-done = bf16[32,2,4608]{2,1,0:T(2,128)(2,1)S(1)} async-done(((bf16[32,2,4608]{2,1,0:T(2,128)(2,1)}), bf16[32,2,4608]{2,1,0:T(2,128)(2,1)S(1)}, u32[]{:S(2)}, u32[]{:S(2)}) %all-to-all-start) | async-done | bytes 589856 | tf_op jit(solution)/shard_map/while/body/eval_jaxpr/all_to_all | solution.py:126
  993.7 3.7 collective-permute-done
  998.0 54.2 %all-gather.4 = bf16[32,2,4608]{2,1,0:T(2,128)(2,1)S(1)} all-gather(bf16[1,2,4608]{2,1,0:T(2,128)(2,1)S(1)} %convert_bitcast_fusion.3), channel_id=1, replica_groups=mesh['section'=16,'feat'=32] {'feat'}, dimensions={0}, use_global_device_ids=true | all-gather | bytes 608256 | tf_op jit(solution)/shard_map/while/body/eval_jaxpr/all_gather | solution.py:103
  1056.7 6.1 all-to-all-start
  1064.0 18.7 %all-to-all-done = bf16[32,2,4608]{2,1,0:T(2,128)(2,1)S(1)} async-done(((bf16[32,2,4608]{2,1,0:T(2,128)(2,1)}), bf16[32,2,4608]{2,1,0:T(2,128)(2,1)S(1)}, u32[]{:S(2)}, u32[]{:S(2)}) %all-to-all-start) | async-done | bytes 589856 | tf_op jit(solution)/shard_map/while/body/eval_jaxpr/all_to_all | solution.py:126
  1087.1 3.6 collective-permute-done
  1091.3 54.2 %all-gather.4 = bf16[32,2,4608]{2,1,0:T(2,128)(2,1)S(1)} all-gather(bf16[1,2,4608]{2,1,0:T(2,128)(2,1)S(1)} %convert_bitcast_fusion.3), channel_id=1, replica_groups=mesh['section'=16,'feat'=32] {'feat'}, dimensions={0}, use_global_device_ids=true | all-gather | bytes 608256 | tf_op jit(solution)/shard_map/while/body/eval_jaxpr/all_gather | solution.py:103
  1150.1 6.1 all-to-all-start
  1157.3 18.7 %all-to-all-done = bf16[32,2,4608]{2,1,0:T(2,128)(2,1)S(1)} async-done(((bf16[32,2,4608]{2,1,0:T(2,128)(2,1)}), bf16[32,2,4608]{2,1,0:T(2,128)(2,1)S(1)}, u32[]{:S(2)}, u32[]{:S(2)}) %all-to-all-start) | async-done | bytes 589856 | tf_op jit(solution)/shard_map/while/body/eval_jaxpr/all_to_all | solution.py:126
  1180.5 3.6 collective-permute-done
  1184.7 54.2 %all-gather.4 = bf16[32,2,4608]{2,1,0:T(2,128)(2,1)S(1)} all-gather(bf16[1,2,4608]{2,1,0:T(2,128)(2,1)S(1)} %convert_bitcast_fusion.3), channel_id=1, replica_groups=mesh['section'=16,'feat'=32] {'feat'}, dimensions={0}, use_global_device_ids=true | all-gather | bytes 608256 | tf_op jit(solution)/shard_map/while/body/eval_jaxpr/all_gather | solution.py:103
  1243.5 6.1 all-to-all-start
  1250.7 18.7 %all-to-all-done = bf16[32,2,4608]{2,1,0:T(2,128)(2,1)S(1)} async-done(((bf16[32,2,4608]{2,1,0:T(2,128)(2,1)}), bf16[32,2,4608]{2,1,0:T(2,128)(2,1)S(1)}, u32[]{:S(2)}, u32[]{:S(2)}) %all-to-all-start) | async-done | bytes 589856 | tf_op jit(solution)/shard_map/while/body/eval_jaxpr/all_to_all | solution.py:126
  1273.9 3.6 collective-permute-done
  1278.1 54.2 %all-gather.4 = bf16[32,2,4608]{2,1,0:T(2,128)(2,1)S(1)} all-gather(bf16[1,2,4608]{2,1,0:T(2,128)(2,1)S(1)} %convert_bitcast_fusion.3), channel_id=1, replica_groups=mesh['section'=16,'feat'=32] {'feat'}, dimensions={0}, use_global_device_ids=true | all-gather | bytes 608256 | tf_op jit(solution)/shard_map/while/body/eval_jaxpr/all_gather | solution.py:103
  1336.8 6.1 all-to-all-start
  1344.1 18.7 %all-to-all-done = bf16[32,2,4608]{2,1,0:T(2,128)(2,1)S(1)} async-done(((bf16[32,2,4608]{2,1,0:T(2,128)(2,1)}), bf16[32,2,4608]{2,1,0:T(2,128)(2,1)S(1)}, u32[]{:S(2)}, u32[]{:S(2)}) %all-to-all-start) | async-done | bytes 589856 | tf_op jit(solution)/shard_map/while/body/eval_jaxpr/all_to_all | solution.py:126
  1367.2 3.6 collective-permute-done
  1371.4 54.2 %all-gather.4 = bf16[32,2,4608]{2,1,0:T(2,128)(2,1)S(1)} all-gather(bf16[1,2,4608]{2,1,0:T(2,128)(2,1)S(1)} %convert_bitcast_fusion.3), channel_id=1, replica_groups=mesh['section'=16,'feat'=32] {'feat'}, dimensions={0}, use_global_device_ids=true | all-gather | bytes 608256 | tf_op jit(solution)/shard_map/while/body/eval_jaxpr/all_gather | solution.py:103
  1430.2 6.1 all-to-all-start
  1437.5 18.7 %all-to-all-done = bf16[32,2,4608]{2,1,0:T(2,128)(2,1)S(1)} async-done(((bf16[32,2,4608]{2,1,0:T(2,128)(2,1)}), bf16[32,2,4608]{2,1,0:T(2,128)(2,1)S(1)}, u32[]{:S(2)}, u32[]{:S(2)}) %all-to-all-start) | async-done | bytes 589856 | tf_op jit(solution)/shard_map/while/body/eval_jaxpr/all_to_all | solution.py:126
  1460.6 3.6 collective-permute-done
  1464.8 54.2 %all-gather.4 = bf16[32,2,4608]{2,1,0:T(2,128)(2,1)S(1)} all-gather(bf16[1,2,4608]{2,1,0:T(2,128)(2,1)S(1)} %convert_bitcast_fusion.3), channel_id=1, replica_groups=mesh['section'=16,'feat'=32] {'feat'}, dimensions={0}, use_global_device_ids=true | all-gather | bytes 608256 | tf_op jit(solution)/shard_map/while/body/eval_jaxpr/all_gather | solution.py:103
  1523.5 6.1 all-to-all-start
  1530.8 18.7 %all-to-all-done = bf16[32,2,4608]{2,1,0:T(2,128)(2,1)S(1)} async-done(((bf16[32,2,4608]{2,1,0:T(2,128)(2,1)}), bf16[32,2,4608]{2,1,0:T(2,128)(2,1)S(1)}, u32[]{:S(2)}, u32[]{:S(2)}) %all-to-all-start) | async-done | bytes 589856 | tf_op jit(solution)/shard_map/while/body/eval_jaxpr/all_to_all | solution.py:126
  1554.0 3.6 collective-permute-done
  1558.2 54.2 %all-gather.4 = bf16[32,2,4608]{2,1,0:T(2,128)(2,1)S(1)} all-gather(bf16[1,2,4608]{2,1,0:T(2,128)(2,1)S(1)} %convert_bitcast_fusion.3), channel_id=1, replica_groups=mesh['section'=16,'feat'=32] {'feat'}, dimensions={0}, use_global_device_ids=true | all-gather | bytes 608256 | tf_op jit(solution)/shard_map/while/body/eval_jaxpr/all_gather | solution.py:103
  1616.9 6.1 all-to-all-start
  1624.2 18.7 %all-to-all-done = bf16[32,2,4608]{2,1,0:T(2,128)(2,1)S(1)} async-done(((bf16[32,2,4608]{2,1,0:T(2,128)(2,1)}), bf16[32,2,4608]{2,1,0:T(2,128)(2,1)S(1)}, u32[]{:S(2)}, u32[]{:S(2)}) %all-to-all-start) | async-done | bytes 589856 | tf_op jit(solution)/shard_map/while/body/eval_jaxpr/all_to_all | solution.py:126
  1647.4 3.6 collective-permute-done
  1651.0 54.2 %all-gather.1 = bf16[32,2,4608]{2,1,0:T(2,128)(2,1)S(1)} all-gather(bf16[1,2,4608]{2,1,0:T(2,128)(2,1)S(1)} %convert_bitcast_fusion.1), channel_id=1, replica_groups=mesh['section'=16,'feat'=32] {'feat'}, dimensions={0}, use_global_device_ids=true | all-gather | bytes 608256 | tf_op jit(solution)/shard_map/all_gather | solution.py:103
  (312 shorter events, 185.6 us)
Async XLA Ops:
  0.0 3.8 copy-start
  7.6 16.5 copy-start.5
  7.6 231.2 %all-to-all-start.1 = ((bf16[32,8,4608]{2,1,0:T(8,128)(2,1)}), bf16[32,8,4608]{2,1,0:T(8,128)(2,1)S(1)}, u32[]{:S(2)}, u32[]{:S(2)}) async-start(bf16[32,8,4608]{2,1,0:T(8,128)(2,1)} %fusion.7), calls=%async_computation.1 | async-start | bytes 4718592 | tf_op jit(solution)/shard_map/all_to_all | solution.py:69
  241.0 2.1 copy-start.2
  243.1 0.6 copy-start.3
  301.2 2.0 copy-start.1
  304.7 30.6 %all-to-all-start = ((bf16[32,2,4608]{2,1,0:T(2,128)(2,1)}), bf16[32,2,4608]{2,1,0:T(2,128)(2,1)S(1)}, u32[]{:S(2)}, u32[]{:S(2)}) async-start(bf16[32,2,4608]{2,1,0:T(2,128)(2,1)} %reshape.317), calls=%async_computation | async-start | bytes 1179648 | tf_op jit(solution)/shard_map/while/body/eval_jaxpr/all_to_all | solution.py:126
  336.6 6.8 collective-permute-start
  343.4 0.6 copy-start.3
  398.4 2.0 copy-start.1
  402.0 27.0 %all-to-all-start = ((bf16[32,2,4608]{2,1,0:T(2,128)(2,1)}), bf16[32,2,4608]{2,1,0:T(2,128)(2,1)S(1)}, u32[]{:S(2)}, u32[]{:S(2)}) async-start(bf16[32,2,4608]{2,1,0:T(2,128)(2,1)} %reshape.317), calls=%async_computation | async-start | bytes 1179648 | tf_op jit(solution)/shard_map/while/body/eval_jaxpr/all_to_all | solution.py:126
  430.3 6.8 collective-permute-start
  437.1 0.6 copy-start.3
  492.8 2.0 copy-start.1
  496.3 26.1 %all-to-all-start = ((bf16[32,2,4608]{2,1,0:T(2,128)(2,1)}), bf16[32,2,4608]{2,1,0:T(2,128)(2,1)S(1)}, u32[]{:S(2)}, u32[]{:S(2)}) async-start(bf16[32,2,4608]{2,1,0:T(2,128)(2,1)} %reshape.317), calls=%async_computation | async-start | bytes 1179648 | tf_op jit(solution)/shard_map/while/body/eval_jaxpr/all_to_all | solution.py:126
  523.7 6.8 collective-permute-start
  530.5 0.6 copy-start.3
  586.2 2.0 copy-start.1
  589.7 26.1 %all-to-all-start = ((bf16[32,2,4608]{2,1,0:T(2,128)(2,1)}), bf16[32,2,4608]{2,1,0:T(2,128)(2,1)S(1)}, u32[]{:S(2)}, u32[]{:S(2)}) async-start(bf16[32,2,4608]{2,1,0:T(2,128)(2,1)} %reshape.317), calls=%async_computation | async-start | bytes 1179648 | tf_op jit(solution)/shard_map/while/body/eval_jaxpr/all_to_all | solution.py:126
  617.1 6.8 collective-permute-start
  623.9 0.6 copy-start.3
  679.6 2.0 copy-start.1
  683.1 26.0 %all-to-all-start = ((bf16[32,2,4608]{2,1,0:T(2,128)(2,1)}), bf16[32,2,4608]{2,1,0:T(2,128)(2,1)S(1)}, u32[]{:S(2)}, u32[]{:S(2)}) async-start(bf16[32,2,4608]{2,1,0:T(2,128)(2,1)} %reshape.317), calls=%async_computation | async-start | bytes 1179648 | tf_op jit(solution)/shard_map/while/body/eval_jaxpr/all_to_all | solution.py:126
  710.4 6.8 collective-permute-start
  717.2 0.6 copy-start.3
  773.0 2.0 copy-start.1
  776.6 25.9 %all-to-all-start = ((bf16[32,2,4608]{2,1,0:T(2,128)(2,1)}), bf16[32,2,4608]{2,1,0:T(2,128)(2,1)S(1)}, u32[]{:S(2)}, u32[]{:S(2)}) async-start(bf16[32,2,4608]{2,1,0:T(2,128)(2,1)} %reshape.317), calls=%async_computation | async-start | bytes 1179648 | tf_op jit(solution)/shard_map/while/body/eval_jaxpr/all_to_all | solution.py:126
  803.8 6.8 collective-permute-start
  810.6 0.6 copy-start.3
  866.4 2.0 copy-start.1
  870.0 25.9 %all-to-all-start = ((bf16[32,2,4608]{2,1,0:T(2,128)(2,1)}), bf16[32,2,4608]{2,1,0:T(2,128)(2,1)S(1)}, u32[]{:S(2)}, u32[]{:S(2)}) async-start(bf16[32,2,4608]{2,1,0:T(2,128)(2,1)} %reshape.317), calls=%async_computation | async-start | bytes 1179648 | tf_op jit(solution)/shard_map/while/body/eval_jaxpr/all_to_all | solution.py:126
  897.2 6.8 collective-permute-start
  904.0 0.6 copy-start.3
  959.7 2.0 copy-start.1
  963.3 26.0 %all-to-all-start = ((bf16[32,2,4608]{2,1,0:T(2,128)(2,1)}), bf16[32,2,4608]{2,1,0:T(2,128)(2,1)S(1)}, u32[]{:S(2)}, u32[]{:S(2)}) async-start(bf16[32,2,4608]{2,1,0:T(2,128)(2,1)} %reshape.317), calls=%async_computation | async-start | bytes 1179648 | tf_op jit(solution)/shard_map/while/body/eval_jaxpr/all_to_all | solution.py:126
  990.5 6.8 collective-permute-start
  997.4 0.6 copy-start.3
  1053.1 2.0 copy-start.1
  1056.7 25.9 %all-to-all-start = ((bf16[32,2,4608]{2,1,0:T(2,128)(2,1)}), bf16[32,2,4608]{2,1,0:T(2,128)(2,1)S(1)}, u32[]{:S(2)}, u32[]{:S(2)}) async-start(bf16[32,2,4608]{2,1,0:T(2,128)(2,1)} %reshape.317), calls=%async_computation | async-start | bytes 1179648 | tf_op jit(solution)/shard_map/while/body/eval_jaxpr/all_to_all | solution.py:126
  1083.9 6.8 collective-permute-start
  1090.7 0.6 copy-start.3
  1146.5 2.0 copy-start.1
  1150.1 26.0 %all-to-all-start = ((bf16[32,2,4608]{2,1,0:T(2,128)(2,1)}), bf16[32,2,4608]{2,1,0:T(2,128)(2,1)S(1)}, u32[]{:S(2)}, u32[]{:S(2)}) async-start(bf16[32,2,4608]{2,1,0:T(2,128)(2,1)} %reshape.317), calls=%async_computation | async-start | bytes 1179648 | tf_op jit(solution)/shard_map/while/body/eval_jaxpr/all_to_all | solution.py:126
  1177.3 6.8 collective-permute-start
  1184.1 0.6 copy-start.3
  1239.9 2.0 copy-start.1
  1243.5 25.9 %all-to-all-start = ((bf16[32,2,4608]{2,1,0:T(2,128)(2,1)}), bf16[32,2,4608]{2,1,0:T(2,128)(2,1)S(1)}, u32[]{:S(2)}, u32[]{:S(2)}) async-start(bf16[32,2,4608]{2,1,0:T(2,128)(2,1)} %reshape.317), calls=%async_computation | async-start | bytes 1179648 | tf_op jit(solution)/shard_map/while/body/eval_jaxpr/all_to_all | solution.py:126
  1270.7 6.8 collective-permute-start
  1277.5 0.6 copy-start.3
  1333.2 2.0 copy-start.1
  1336.8 26.0 %all-to-all-start = ((bf16[32,2,4608]{2,1,0:T(2,128)(2,1)}), bf16[32,2,4608]{2,1,0:T(2,128)(2,1)S(1)}, u32[]{:S(2)}, u32[]{:S(2)}) async-start(bf16[32,2,4608]{2,1,0:T(2,128)(2,1)} %reshape.317), calls=%async_computation | async-start | bytes 1179648 | tf_op jit(solution)/shard_map/while/body/eval_jaxpr/all_to_all | solution.py:126
  1364.0 6.8 collective-permute-start
  1370.8 0.6 copy-start.3
  1426.6 2.0 copy-start.1
  1430.2 25.9 %all-to-all-start = ((bf16[32,2,4608]{2,1,0:T(2,128)(2,1)}), bf16[32,2,4608]{2,1,0:T(2,128)(2,1)S(1)}, u32[]{:S(2)}, u32[]{:S(2)}) async-start(bf16[32,2,4608]{2,1,0:T(2,128)(2,1)} %reshape.317), calls=%async_computation | async-start | bytes 1179648 | tf_op jit(solution)/shard_map/while/body/eval_jaxpr/all_to_all | solution.py:126
  1457.4 6.8 collective-permute-start
  1464.2 0.6 copy-start.3
  1520.0 2.0 copy-start.1
  1523.5 26.0 %all-to-all-start = ((bf16[32,2,4608]{2,1,0:T(2,128)(2,1)}), bf16[32,2,4608]{2,1,0:T(2,128)(2,1)S(1)}, u32[]{:S(2)}, u32[]{:S(2)}) async-start(bf16[32,2,4608]{2,1,0:T(2,128)(2,1)} %reshape.317), calls=%async_computation | async-start | bytes 1179648 | tf_op jit(solution)/shard_map/while/body/eval_jaxpr/all_to_all | solution.py:126
  1550.8 6.8 collective-permute-start
  1613.4 2.0 copy-start.1
  1616.9 25.9 %all-to-all-start = ((bf16[32,2,4608]{2,1,0:T(2,128)(2,1)}), bf16[32,2,4608]{2,1,0:T(2,128)(2,1)S(1)}, u32[]{:S(2)}, u32[]{:S(2)}) async-start(bf16[32,2,4608]{2,1,0:T(2,128)(2,1)} %reshape.317), calls=%async_computation | async-start | bytes 1179648 | tf_op jit(solution)/shard_map/while/body/eval_jaxpr/all_to_all | solution.py:126
  1644.1 6.8 collective-permute-start
  1705.4 1.9 copy-start.4
  (1 other events, 0.6 us)
where the time goes:
time: 1710 us
  blocking collectives  1070 us (63%)
  waiting for transfers between devices  334 us (20%)
  starting transfers between devices  143 us (8%)
  other arithmetic  60.3 us (4%)
  matrix products  49.9 us (3%)
  local copies, waits for them, and re-layouts  46.1 us (3%)
    all_gather x16, blocking collectives, gathered_products(): lax.all_gather(adjoint_rows.astype(jnp.bfloat16), 'feat', axis=0, tiled=T...  868 us
    all_to_all x15, waiting for transfers between devices, propagate(): lax.all_to_all(head_term.reshape(feat_count, rows_dev, model_width), 'fea...  281 us
    psum x1, blocking collectives, per_device(): lax.psum(enc_part.astype(jnp.bfloat16), 'feat').astype(jnp.float32)  205 us
    all_to_all x15, starting transfers between devices, propagate(): lax.all_to_all(head_term.reshape(feat_count, rows_dev, model_width), 'fea...  97.3 us
    ppermute x15, waiting for transfers between devices, shifted(): return lax.ppermute(shard, axis, pairs)  53.8 us
  transfers between devices with their start and end apart: 31, of which 30 were waited for; matrix products, arithmetic and copies ran while one was open for 3% of the time, Pallas kernels for 0%

commit v1 on v0

--- a/solution.py
+++ b/solution.py
@@ -75,7 +75,9 @@
         jnp.bfloat16
     )
     enc_part = jnp.dot(target_pick, enc_table, preferred_element_type=jnp.float32)
-    enc_full = lax.psum(enc_part.astype(jnp.bfloat16), "feat").astype(jnp.float32)
+    enc_full = jnp.sum(lax.all_gather(enc_part.astype(jnp.bfloat16), "feat"), axis=0).astype(
+        jnp.float32
+    )
     row_iota = feat_index * rows_dev + jnp.arange(rows_dev, dtype=jnp.int32)
     row_target = row_iota // seq_len
     row_pos = row_iota % seq_len

time: 1710 us -> 1630 us (0.953)
  blocking collectives: 1070 us -> 861 us
  waiting for transfers between devices: 334 us -> 451 us
    psum x1 -> x0, blocking collectives: 205 us -> none  [per_device(): lax.psum(enc_part.astype(jnp.bfloat16), 'feat').astype(jnp.float32)]
    all_gather x0 -> x1, waiting for transfers between devices: none -> 117 us  [per_device(): lax.all_gather(enc_part.astype(jnp.bfloat16), 'feat')]
  transfers between devices with their start and end apart: 31 -> 32, of which waited for: 30 -> 31; matrix products, arithmetic and copies ran while one was open for 3% -> 3% of each run, Pallas kernels for 0% -> 0%
where the time goes in v1:
time: 1630 us
  blocking collectives  861 us (53%)
  waiting for transfers between devices  451 us (28%)
  starting transfers between devices  141 us (9%)
  other arithmetic  62.5 us (4%)
  matrix products  50 us (3%)
  local copies, waits for them, and re-layouts  46.1 us (3%)
    all_gather x16, blocking collectives, gathered_products(): lax.all_gather(adjoint_rows.astype(jnp.bfloat16), 'feat', axis=0, tiled=T...  861 us
    all_to_all x15, waiting for transfers between devices, propagate(): lax.all_to_all(head_term.reshape(feat_count, rows_dev, model_width), 'fea...  280 us
    all_gather x1, waiting for transfers between devices, per_device(): lax.all_gather(enc_part.astype(jnp.bfloat16), 'feat')  117 us
    all_to_all x15, starting transfers between devices, propagate(): lax.all_to_all(head_term.reshape(feat_count, rows_dev, model_width), 'fea...  95.1 us
    ppermute x15, waiting for transfers between devices, shifted(): return lax.ppermute(shard, axis, pairs)  53.8 us
  transfers between devices with their start and end apart: 32, of which 31 were waited for; matrix products, arithmetic and copies ran while one was open for 3% of the time, Pallas kernels for 0%

profile of v1, /device:TPU:7, one launch (start us, length us, event | category | flops | bytes accessed | tf_op | source)
XLA Modules:
  0.0 1625.2 jit_solution(17540477301843990398)
XLA Ops:
  14.1 16.5 %all-to-all-start.1 = ((bf16[32,8,4608]{2,1,0:T(8,128)(2,1)}), bf16[32,8,4608]{2,1,0:T(8,128)(2,1)S(1)}, u32[]{:S(2)}, u32[]{:S(2)}) async-start(bf16[32,8,4608]{2,1,0:T(8,128)(2,1)} %fusion.8), calls=%async_computation.1 | async-start | bytes 4718592 | tf_op jit(solution)/shard_map/all_to_all | solution.py:69
  38.3 116.7 %all-gather.9.cloned.1.call-done = bf16[32,4,4608]{2,1,0:T(4,128)(2,1)} async-done(((bf16[1,4,4608]{2,1,0:T(4,128)(2,1)}), bf16[32,4,4608]{2,1,0:T(4,128)(2,1)}) %all-gather.9.cloned.1.call-update) | async-done | bytes 1179664 | tf_op jit(solution)/shard_map/all_gather | solution.py:78
  163.3 1397.4 %while.16 = (s32[]{:T(128)}, f32[2,4608]{1,0:T(2,128)S(1)}, f32[64,128]{1,0:T(8,128)}, bf16[128,4608]{1,0:T(8,128)(2,1)}, bf16[16,16]{0,1:T(8,128)(2,1)S(1)}, /*...) while((s32[]{:T(128)}, f32[2,4608]{1,0:T(2,128)S(1)}, ...), condition=%wide.region_9.10_spmd.clone, body=%wide.region_6.9_spmd.clone.sunk | while | flops 227964416 | bytes 15944625 | solution.py:146
  163.9 48.1 %all-gather.6 = bf16[32,2,4608]{2,1,0:T(2,128)(2,1)S(1)} all-gather(bf16[1,2,4608]{2,1,0:T(2,128)(2,1)S(1)} %convert_bitcast_fusion.3), channel_id=1, replica_groups=mesh['section'=16,'feat'=32] {'feat'}, dimensions={0}, use_global_device_ids=true | all-gather | bytes 608256 | tf_op jit(solution)/shard_map/while/body/eval_jaxpr/all_gather | solution.py:105
  216.6 9.1 all-to-all-start
  226.8 18.5 %all-to-all-done = bf16[32,2,4608]{2,1,0:T(2,128)(2,1)S(1)} async-done(((bf16[32,2,4608]{2,1,0:T(2,128)(2,1)}), bf16[32,2,4608]{2,1,0:T(2,128)(2,1)S(1)}, u32[]{:S(2)}, u32[]{:S(2)}) %all-to-all-start) | async-done | bytes 589856 | tf_op jit(solution)/shard_map/while/body/eval_jaxpr/all_to_all | solution.py:128
  250.4 3.0 collective-permute-done
  254.0 54.0 %all-gather.6 = bf16[32,2,4608]{2,1,0:T(2,128)(2,1)S(1)} all-gather(bf16[1,2,4608]{2,1,0:T(2,128)(2,1)S(1)} %convert_bitcast_fusion.3), channel_id=1, replica_groups=mesh['section'=16,'feat'=32] {'feat'}, dimensions={0}, use_global_device_ids=true | all-gather | bytes 608256 | tf_op jit(solution)/shard_map/while/body/eval_jaxpr/all_gather | solution.py:105
  312.6 6.3 all-to-all-start
  320.1 18.7 %all-to-all-done = bf16[32,2,4608]{2,1,0:T(2,128)(2,1)S(1)} async-done(((bf16[32,2,4608]{2,1,0:T(2,128)(2,1)}), bf16[32,2,4608]{2,1,0:T(2,128)(2,1)S(1)}, u32[]{:S(2)}, u32[]{:S(2)}) %all-to-all-start) | async-done | bytes 589856 | tf_op jit(solution)/shard_map/while/body/eval_jaxpr/all_to_all | solution.py:128
  343.2 3.6 collective-permute-done
  347.5 54.1 %all-gather.6 = bf16[32,2,4608]{2,1,0:T(2,128)(2,1)S(1)} all-gather(bf16[1,2,4608]{2,1,0:T(2,128)(2,1)S(1)} %convert_bitcast_fusion.3), channel_id=1, replica_groups=mesh['section'=16,'feat'=32] {'feat'}, dimensions={0}, use_global_device_ids=true | all-gather | bytes 608256 | tf_op jit(solution)/shard_map/while/body/eval_jaxpr/all_gather | solution.py:105
  406.1 6.2 all-to-all-start
  413.5 18.7 %all-to-all-done = bf16[32,2,4608]{2,1,0:T(2,128)(2,1)S(1)} async-done(((bf16[32,2,4608]{2,1,0:T(2,128)(2,1)}), bf16[32,2,4608]{2,1,0:T(2,128)(2,1)S(1)}, u32[]{:S(2)}, u32[]{:S(2)}) %all-to-all-start) | async-done | bytes 589856 | tf_op jit(solution)/shard_map/while/body/eval_jaxpr/all_to_all | solution.py:128
  436.6 3.6 collective-permute-done
  440.8 54.1 %all-gather.6 = bf16[32,2,4608]{2,1,0:T(2,128)(2,1)S(1)} all-gather(bf16[1,2,4608]{2,1,0:T(2,128)(2,1)S(1)} %convert_bitcast_fusion.3), channel_id=1, replica_groups=mesh['section'=16,'feat'=32] {'feat'}, dimensions={0}, use_global_device_ids=true | all-gather | bytes 608256 | tf_op jit(solution)/shard_map/while/body/eval_jaxpr/all_gather | solution.py:105
  499.5 6.2 all-to-all-start
  506.9 18.7 %all-to-all-done = bf16[32,2,4608]{2,1,0:T(2,128)(2,1)S(1)} async-done(((bf16[32,2,4608]{2,1,0:T(2,128)(2,1)}), bf16[32,2,4608]{2,1,0:T(2,128)(2,1)S(1)}, u32[]{:S(2)}, u32[]{:S(2)}) %all-to-all-start) | async-done | bytes 589856 | tf_op jit(solution)/shard_map/while/body/eval_jaxpr/all_to_all | solution.py:128
  530.0 3.6 collective-permute-done
  534.2 54.2 %all-gather.6 = bf16[32,2,4608]{2,1,0:T(2,128)(2,1)S(1)} all-gather(bf16[1,2,4608]{2,1,0:T(2,128)(2,1)S(1)} %convert_bitcast_fusion.3), channel_id=1, replica_groups=mesh['section'=16,'feat'=32] {'feat'}, dimensions={0}, use_global_device_ids=true | all-gather | bytes 608256 | tf_op jit(solution)/shard_map/while/body/eval_jaxpr/all_gather | solution.py:105
  593.0 6.1 all-to-all-start
  600.2 18.7 %all-to-all-done = bf16[32,2,4608]{2,1,0:T(2,128)(2,1)S(1)} async-done(((bf16[32,2,4608]{2,1,0:T(2,128)(2,1)}), bf16[32,2,4608]{2,1,0:T(2,128)(2,1)S(1)}, u32[]{:S(2)}, u32[]{:S(2)}) %all-to-all-start) | async-done | bytes 589856 | tf_op jit(solution)/shard_map/while/body/eval_jaxpr/all_to_all | solution.py:128
  623.4 3.6 collective-permute-done
  627.6 54.2 %all-gather.6 = bf16[32,2,4608]{2,1,0:T(2,128)(2,1)S(1)} all-gather(bf16[1,2,4608]{2,1,0:T(2,128)(2,1)S(1)} %convert_bitcast_fusion.3), channel_id=1, replica_groups=mesh['section'=16,'feat'=32] {'feat'}, dimensions={0}, use_global_device_ids=true | all-gather | bytes 608256 | tf_op jit(solution)/shard_map/while/body/eval_jaxpr/all_gather | solution.py:105
  686.3 6.1 all-to-all-start
  693.6 18.7 %all-to-all-done = bf16[32,2,4608]{2,1,0:T(2,128)(2,1)S(1)} async-done(((bf16[32,2,4608]{2,1,0:T(2,128)(2,1)}), bf16[32,2,4608]{2,1,0:T(2,128)(2,1)S(1)}, u32[]{:S(2)}, u32[]{:S(2)}) %all-to-all-start) | async-done | bytes 589856 | tf_op jit(solution)/shard_map/while/body/eval_jaxpr/all_to_all | solution.py:128
  716.7 3.7 collective-permute-done
  721.0 54.2 %all-gather.6 = bf16[32,2,4608]{2,1,0:T(2,128)(2,1)S(1)} all-gather(bf16[1,2,4608]{2,1,0:T(2,128)(2,1)S(1)} %convert_bitcast_fusion.3), channel_id=1, replica_groups=mesh['section'=16,'feat'=32] {'feat'}, dimensions={0}, use_global_device_ids=true | all-gather | bytes 608256 | tf_op jit(solution)/shard_map/while/body/eval_jaxpr/all_gather | solution.py:105
  779.7 6.1 all-to-all-start
  787.0 18.7 %all-to-all-done = bf16[32,2,4608]{2,1,0:T(2,128)(2,1)S(1)} async-done(((bf16[32,2,4608]{2,1,0:T(2,128)(2,1)}), bf16[32,2,4608]{2,1,0:T(2,128)(2,1)S(1)}, u32[]{:S(2)}, u32[]{:S(2)}) %all-to-all-start) | async-done | bytes 589856 | tf_op jit(solution)/shard_map/while/body/eval_jaxpr/all_to_all | solution.py:128
  810.1 3.6 collective-permute-done
  814.3 54.2 %all-gather.6 = bf16[32,2,4608]{2,1,0:T(2,128)(2,1)S(1)} all-gather(bf16[1,2,4608]{2,1,0:T(2,128)(2,1)S(1)} %convert_bitcast_fusion.3), channel_id=1, replica_groups=mesh['section'=16,'feat'=32] {'feat'}, dimensions={0}, use_global_device_ids=true | all-gather | bytes 608256 | tf_op jit(solution)/shard_map/while/body/eval_jaxpr/all_gather | solution.py:105
  873.1 6.1 all-to-all-start
  880.3 18.7 %all-to-all-done = bf16[32,2,4608]{2,1,0:T(2,128)(2,1)S(1)} async-done(((bf16[32,2,4608]{2,1,0:T(2,128)(2,1)}), bf16[32,2,4608]{2,1,0:T(2,128)(2,1)S(1)}, u32[]{:S(2)}, u32[]{:S(2)}) %all-to-all-start) | async-done | bytes 589856 | tf_op jit(solution)/shard_map/while/body/eval_jaxpr/all_to_all | solution.py:128
  903.4 3.7 collective-permute-done
  907.7 54.2 %all-gather.6 = bf16[32,2,4608]{2,1,0:T(2,128)(2,1)S(1)} all-gather(bf16[1,2,4608]{2,1,0:T(2,128)(2,1)S(1)} %convert_bitcast_fusion.3), channel_id=1, replica_groups=mesh['section'=16,'feat'=32] {'feat'}, dimensions={0}, use_global_device_ids=true | all-gather | bytes 608256 | tf_op jit(solution)/shard_map/while/body/eval_jaxpr/all_gather | solution.py:105
  966.4 6.1 all-to-all-start
  973.7 18.7 %all-to-all-done = bf16[32,2,4608]{2,1,0:T(2,128)(2,1)S(1)} async-done(((bf16[32,2,4608]{2,1,0:T(2,128)(2,1)}), bf16[32,2,4608]{2,1,0:T(2,128)(2,1)S(1)}, u32[]{:S(2)}, u32[]{:S(2)}) %all-to-all-start) | async-done | bytes 589856 | tf_op jit(solution)/shard_map/while/body/eval_jaxpr/all_to_all | solution.py:128
  996.8 3.6 collective-permute-done
  1001.1 54.2 %all-gather.6 = bf16[32,2,4608]{2,1,0:T(2,128)(2,1)S(1)} all-gather(bf16[1,2,4608]{2,1,0:T(2,128)(2,1)S(1)} %convert_bitcast_fusion.3), channel_id=1, replica_groups=mesh['section'=16,'feat'=32] {'feat'}, dimensions={0}, use_global_device_ids=true | all-gather | bytes 608256 | tf_op jit(solution)/shard_map/while/body/eval_jaxpr/all_gather | solution.py:105
  1059.8 6.1 all-to-all-start
  1067.1 18.7 %all-to-all-done = bf16[32,2,4608]{2,1,0:T(2,128)(2,1)S(1)} async-done(((bf16[32,2,4608]{2,1,0:T(2,128)(2,1)}), bf16[32,2,4608]{2,1,0:T(2,128)(2,1)S(1)}, u32[]{:S(2)}, u32[]{:S(2)}) %all-to-all-start) | async-done | bytes 589856 | tf_op jit(solution)/shard_map/while/body/eval_jaxpr/all_to_all | solution.py:128
  1090.2 3.6 collective-permute-done
  1094.5 54.2 %all-gather.6 = bf16[32,2,4608]{2,1,0:T(2,128)(2,1)S(1)} all-gather(bf16[1,2,4608]{2,1,0:T(2,128)(2,1)S(1)} %convert_bitcast_fusion.3), channel_id=1, replica_groups=mesh['section'=16,'feat'=32] {'feat'}, dimensions={0}, use_global_device_ids=true | all-gather | bytes 608256 | tf_op jit(solution)/shard_map/while/body/eval_jaxpr/all_gather | solution.py:105
  1153.2 6.1 all-to-all-start
  1160.5 18.7 %all-to-all-done = bf16[32,2,4608]{2,1,0:T(2,128)(2,1)S(1)} async-done(((bf16[32,2,4608]{2,1,0:T(2,128)(2,1)}), bf16[32,2,4608]{2,1,0:T(2,128)(2,1)S(1)}, u32[]{:S(2)}, u32[]{:S(2)}) %all-to-all-start) | async-done | bytes 589856 | tf_op jit(solution)/shard_map/while/body/eval_jaxpr/all_to_all | solution.py:128
  1183.6 3.6 collective-permute-done
  1187.8 54.2 %all-gather.6 = bf16[32,2,4608]{2,1,0:T(2,128)(2,1)S(1)} all-gather(bf16[1,2,4608]{2,1,0:T(2,128)(2,1)S(1)} %convert_bitcast_fusion.3), channel_id=1, replica_groups=mesh['section'=16,'feat'=32] {'feat'}, dimensions={0}, use_global_device_ids=true | all-gather | bytes 608256 | tf_op jit(solution)/shard_map/while/body/eval_jaxpr/all_gather | solution.py:105
  1246.6 6.1 all-to-all-start
  1253.8 18.7 %all-to-all-done = bf16[32,2,4608]{2,1,0:T(2,128)(2,1)S(1)} async-done(((bf16[32,2,4608]{2,1,0:T(2,128)(2,1)}), bf16[32,2,4608]{2,1,0:T(2,128)(2,1)S(1)}, u32[]{:S(2)}, u32[]{:S(2)}) %all-to-all-start) | async-done | bytes 589856 | tf_op jit(solution)/shard_map/while/body/eval_jaxpr/all_to_all | solution.py:128
  1277.0 3.6 collective-permute-done
  1281.2 54.2 %all-gather.6 = bf16[32,2,4608]{2,1,0:T(2,128)(2,1)S(1)} all-gather(bf16[1,2,4608]{2,1,0:T(2,128)(2,1)S(1)} %convert_bitcast_fusion.3), channel_id=1, replica_groups=mesh['section'=16,'feat'=32] {'feat'}, dimensions={0}, use_global_device_ids=true | all-gather | bytes 608256 | tf_op jit(solution)/shard_map/while/body/eval_jaxpr/all_gather | solution.py:105
  1339.9 6.1 all-to-all-start
  1347.2 18.7 %all-to-all-done = bf16[32,2,4608]{2,1,0:T(2,128)(2,1)S(1)} async-done(((bf16[32,2,4608]{2,1,0:T(2,128)(2,1)}), bf16[32,2,4608]{2,1,0:T(2,128)(2,1)S(1)}, u32[]{:S(2)}, u32[]{:S(2)}) %all-to-all-start) | async-done | bytes 589856 | tf_op jit(solution)/shard_map/while/body/eval_jaxpr/all_to_all | solution.py:128
  1370.4 3.6 collective-permute-done
  1374.6 54.2 %all-gather.6 = bf16[32,2,4608]{2,1,0:T(2,128)(2,1)S(1)} all-gather(bf16[1,2,4608]{2,1,0:T(2,128)(2,1)S(1)} %convert_bitcast_fusion.3), channel_id=1, replica_groups=mesh['section'=16,'feat'=32] {'feat'}, dimensions={0}, use_global_device_ids=true | all-gather | bytes 608256 | tf_op jit(solution)/shard_map/while/body/eval_jaxpr/all_gather | solution.py:105
  1433.3 6.1 all-to-all-start
  1440.6 18.7 %all-to-all-done = bf16[32,2,4608]{2,1,0:T(2,128)(2,1)S(1)} async-done(((bf16[32,2,4608]{2,1,0:T(2,128)(2,1)}), bf16[32,2,4608]{2,1,0:T(2,128)(2,1)S(1)}, u32[]{:S(2)}, u32[]{:S(2)}) %all-to-all-start) | async-done | bytes 589856 | tf_op jit(solution)/shard_map/while/body/eval_jaxpr/all_to_all | solution.py:128
  1463.7 3.6 collective-permute-done
  1467.9 54.2 %all-gather.6 = bf16[32,2,4608]{2,1,0:T(2,128)(2,1)S(1)} all-gather(bf16[1,2,4608]{2,1,0:T(2,128)(2,1)S(1)} %convert_bitcast_fusion.3), channel_id=1, replica_groups=mesh['section'=16,'feat'=32] {'feat'}, dimensions={0}, use_global_device_ids=true | all-gather | bytes 608256 | tf_op jit(solution)/shard_map/while/body/eval_jaxpr/all_gather | solution.py:105
  1526.7 6.1 all-to-all-start
  1534.0 18.7 %all-to-all-done = bf16[32,2,4608]{2,1,0:T(2,128)(2,1)S(1)} async-done(((bf16[32,2,4608]{2,1,0:T(2,128)(2,1)}), bf16[32,2,4608]{2,1,0:T(2,128)(2,1)S(1)}, u32[]{:S(2)}, u32[]{:S(2)}) %all-to-all-start) | async-done | bytes 589856 | tf_op jit(solution)/shard_map/while/body/eval_jaxpr/all_to_all | solution.py:128
  1557.1 3.6 collective-permute-done
  1560.7 54.2 %all-gather.3 = bf16[32,2,4608]{2,1,0:T(2,128)(2,1)S(1)} all-gather(bf16[1,2,4608]{2,1,0:T(2,128)(2,1)S(1)} %convert_bitcast_fusion.1), channel_id=1, replica_groups=mesh['section'=16,'feat'=32] {'feat'}, dimensions={0}, use_global_device_ids=true | all-gather | bytes 608256 | tf_op jit(solution)/shard_map/all_gather | solution.py:105
  (319 shorter events, 188.0 us)
Async XLA Ops:
  6.5 3.8 copy-start
  14.1 16.6 %copy-start.7 = (s32[4]{0:T(128)S(1)}, s32[4]{0:T(128)}, u32[]{:S(2)}) copy-start(s32[4]{0:T(128)} %param.20) | copy-start | bytes 52
  14.1 144.9 %all-to-all-start.1 = ((bf16[32,8,4608]{2,1,0:T(8,128)(2,1)}), bf16[32,8,4608]{2,1,0:T(8,128)(2,1)S(1)}, u32[]{:S(2)}, u32[]{:S(2)}) async-start(bf16[32,8,4608]{2,1,0:T(8,128)(2,1)} %fusion.8), calls=%async_computation.1 | async-start | bytes 4718592 | tf_op jit(solution)/shard_map/all_to_all | solution.py:69
  30.6 2.3 copy-start.5
  30.6 124.4 %all-gather.9.cloned.1.call-start = ((), (), s32[]{:S(2)}) async-start(), calls=%async_computation.2 | async-start | bytes 1216512 | tf_op jit(solution)/shard_map/all_gather | solution.py:78
  33.0 4.7 copy-start.6
  161.2 2.1 copy-start.2
  163.3 0.6 copy-start.3
  213.0 2.0 copy-start.1
  216.6 28.8 %all-to-all-start = ((bf16[32,2,4608]{2,1,0:T(2,128)(2,1)}), bf16[32,2,4608]{2,1,0:T(2,128)(2,1)S(1)}, u32[]{:S(2)}, u32[]{:S(2)}) async-start(bf16[32,2,4608]{2,1,0:T(2,128)(2,1)} %reshape.321), calls=%async_computation | async-start | bytes 1179648 | tf_op jit(solution)/shard_map/while/body/eval_jaxpr/all_to_all | solution.py:128
  246.6 6.8 collective-permute-start
  253.4 0.6 copy-start.3
  309.1 2.0 copy-start.1
  312.6 26.1 %all-to-all-start = ((bf16[32,2,4608]{2,1,0:T(2,128)(2,1)}), bf16[32,2,4608]{2,1,0:T(2,128)(2,1)S(1)}, u32[]{:S(2)}, u32[]{:S(2)}) async-start(bf16[32,2,4608]{2,1,0:T(2,128)(2,1)} %reshape.321), calls=%async_computation | async-start | bytes 1179648 | tf_op jit(solution)/shard_map/while/body/eval_jaxpr/all_to_all | solution.py:128
  340.1 6.8 collective-permute-start
  346.9 0.6 copy-start.3
  402.5 2.0 copy-start.1
  406.1 26.1 %all-to-all-start = ((bf16[32,2,4608]{2,1,0:T(2,128)(2,1)}), bf16[32,2,4608]{2,1,0:T(2,128)(2,1)S(1)}, u32[]{:S(2)}, u32[]{:S(2)}) async-start(bf16[32,2,4608]{2,1,0:T(2,128)(2,1)} %reshape.321), calls=%async_computation | async-start | bytes 1179648 | tf_op jit(solution)/shard_map/while/body/eval_jaxpr/all_to_all | solution.py:128
  433.4 6.8 collective-permute-start
  440.2 0.6 copy-start.3
  495.9 2.0 copy-start.1
  499.5 26.1 %all-to-all-start = ((bf16[32,2,4608]{2,1,0:T(2,128)(2,1)}), bf16[32,2,4608]{2,1,0:T(2,128)(2,1)S(1)}, u32[]{:S(2)}, u32[]{:S(2)}) async-start(bf16[32,2,4608]{2,1,0:T(2,128)(2,1)} %reshape.321), calls=%async_computation | async-start | bytes 1179648 | tf_op jit(solution)/shard_map/while/body/eval_jaxpr/all_to_all | solution.py:128
  526.8 6.8 collective-permute-start
  533.6 0.6 copy-start.3
  589.4 2.0 copy-start.1
  593.0 25.9 %all-to-all-start = ((bf16[32,2,4608]{2,1,0:T(2,128)(2,1)}), bf16[32,2,4608]{2,1,0:T(2,128)(2,1)S(1)}, u32[]{:S(2)}, u32[]{:S(2)}) async-start(bf16[32,2,4608]{2,1,0:T(2,128)(2,1)} %reshape.321), calls=%async_computation | async-start | bytes 1179648 | tf_op jit(solution)/shard_map/while/body/eval_jaxpr/all_to_all | solution.py:128
  620.2 6.8 collective-permute-start
  627.0 0.6 copy-start.3
  682.8 2.0 copy-start.1
  686.3 25.9 %all-to-all-start = ((bf16[32,2,4608]{2,1,0:T(2,128)(2,1)}), bf16[32,2,4608]{2,1,0:T(2,128)(2,1)S(1)}, u32[]{:S(2)}, u32[]{:S(2)}) async-start(bf16[32,2,4608]{2,1,0:T(2,128)(2,1)} %reshape.321), calls=%async_computation | async-start | bytes 1179648 | tf_op jit(solution)/shard_map/while/body/eval_jaxpr/all_to_all | solution.py:128
  713.5 6.8 collective-permute-start
  720.4 0.6 copy-start.3
  776.1 2.0 copy-start.1
  779.7 26.0 %all-to-all-start = ((bf16[32,2,4608]{2,1,0:T(2,128)(2,1)}), bf16[32,2,4608]{2,1,0:T(2,128)(2,1)S(1)}, u32[]{:S(2)}, u32[]{:S(2)}) async-start(bf16[32,2,4608]{2,1,0:T(2,128)(2,1)} %reshape.321), calls=%async_computation | async-start | bytes 1179648 | tf_op jit(solution)/shard_map/while/body/eval_jaxpr/all_to_all | solution.py:128
  806.9 6.8 collective-permute-start
  813.7 0.6 copy-start.3
  869.5 2.0 copy-start.1
  873.1 25.9 %all-to-all-start = ((bf16[32,2,4608]{2,1,0:T(2,128)(2,1)}), bf16[32,2,4608]{2,1,0:T(2,128)(2,1)S(1)}, u32[]{:S(2)}, u32[]{:S(2)}) async-start(bf16[32,2,4608]{2,1,0:T(2,128)(2,1)} %reshape.321), calls=%async_computation | async-start | bytes 1179648 | tf_op jit(solution)/shard_map/while/body/eval_jaxpr/all_to_all | solution.py:128
  900.3 6.8 collective-permute-start
  907.1 0.6 copy-start.3
  962.9 2.0 copy-start.1
  966.4 26.0 %all-to-all-start = ((bf16[32,2,4608]{2,1,0:T(2,128)(2,1)}), bf16[32,2,4608]{2,1,0:T(2,128)(2,1)S(1)}, u32[]{:S(2)}, u32[]{:S(2)}) async-start(bf16[32,2,4608]{2,1,0:T(2,128)(2,1)} %reshape.321), calls=%async_computation | async-start | bytes 1179648 | tf_op jit(solution)/shard_map/while/body/eval_jaxpr/all_to_all | solution.py:128
  993.7 6.8 collective-permute-start
  1000.5 0.6 copy-start.3
  1056.3 2.0 copy-start.1
  1059.8 25.9 %all-to-all-start = ((bf16[32,2,4608]{2,1,0:T(2,128)(2,1)}), bf16[32,2,4608]{2,1,0:T(2,128)(2,1)S(1)}, u32[]{:S(2)}, u32[]{:S(2)}) async-start(bf16[32,2,4608]{2,1,0:T(2,128)(2,1)} %reshape.321), calls=%async_computation | async-start | bytes 1179648 | tf_op jit(solution)/shard_map/while/body/eval_jaxpr/all_to_all | solution.py:128
  1087.0 6.8 collective-permute-start
  1093.8 0.6 copy-start.3
  1149.6 2.0 copy-start.1
  1153.2 26.0 %all-to-all-start = ((bf16[32,2,4608]{2,1,0:T(2,128)(2,1)}), bf16[32,2,4608]{2,1,0:T(2,128)(2,1)S(1)}, u32[]{:S(2)}, u32[]{:S(2)}) async-start(bf16[32,2,4608]{2,1,0:T(2,128)(2,1)} %reshape.321), calls=%async_computation | async-start | bytes 1179648 | tf_op jit(solution)/shard_map/while/body/eval_jaxpr/all_to_all | solution.py:128
  1180.4 6.8 collective-permute-start
  1243.0 2.0 copy-start.1
  1246.6 25.9 %all-to-all-start = ((bf16[32,2,4608]{2,1,0:T(2,128)(2,1)}), bf16[32,2,4608]{2,1,0:T(2,128)(2,1)S(1)}, u32[]{:S(2)}, u32[]{:S(2)}) async-start(bf16[32,2,4608]{2,1,0:T(2,128)(2,1)} %reshape.321), calls=%async_computation | async-start | bytes 1179648 | tf_op jit(solution)/shard_map/while/body/eval_jaxpr/all_to_all | solution.py:128
  1273.8 6.8 collective-permute-start
  1336.4 2.0 copy-start.1
  1339.9 26.0 %all-to-all-start = ((bf16[32,2,4608]{2,1,0:T(2,128)(2,1)}), bf16[32,2,4608]{2,1,0:T(2,128)(2,1)S(1)}, u32[]{:S(2)}, u32[]{:S(2)}) async-start(bf16[32,2,4608]{2,1,0:T(2,128)(2,1)} %reshape.321), calls=%async_computation | async-start | bytes 1179648 | tf_op jit(solution)/shard_map/while/body/eval_jaxpr/all_to_all | solution.py:128
  1367.2 6.8 collective-permute-start
  1429.7 2.0 copy-start.1
  1433.3 25.9 %all-to-all-start = ((bf16[32,2,4608]{2,1,0:T(2,128)(2,1)}), bf16[32,2,4608]{2,1,0:T(2,128)(2,1)S(1)}, u32[]{:S(2)}, u32[]{:S(2)}) async-start(bf16[32,2,4608]{2,1,0:T(2,128)(2,1)} %reshape.321), calls=%async_computation | async-start | bytes 1179648 | tf_op jit(solution)/shard_map/while/body/eval_jaxpr/all_to_all | solution.py:128
  1460.5 6.8 collective-permute-start
  1523.1 2.0 copy-start.1
  1526.7 26.0 %all-to-all-start = ((bf16[32,2,4608]{2,1,0:T(2,128)(2,1)}), bf16[32,2,4608]{2,1,0:T(2,128)(2,1)S(1)}, u32[]{:S(2)}, u32[]{:S(2)}) async-start(bf16[32,2,4608]{2,1,0:T(2,128)(2,1)} %reshape.321), calls=%async_computation | async-start | bytes 1179648 | tf_op jit(solution)/shard_map/while/body/eval_jaxpr/all_to_all | solution.py:128
  1553.9 6.8 collective-permute-start
  1615.2 1.9 copy-start.4
  (4 other events, 2.4 us)
Sparse Core Ops, SparseCore 0:
  34.7 120.2 all-gather.8
